TPU v7x, 256 devices: a whole 4x4x8 slice. The times are simulated.
256 devices in a mesh: dp: 8 (over y_hi, x), tp: 32 (over z, y_lo, core).
Axes of the slice: x: 4, y: 4 (y_hi: 2, y_lo: 2; y = y_hi * 2 + y_lo), z: 8, core: 2. Of those that a mesh axis runs over, the one named last changes fastest.
Arguments:
- tokens: bfloat16 [4096, 4096], P(('dp', 'tp')), may hold values from -6 to 6
- norm_scale_vector: float32 [4096], replicated, may hold values from 0.5 to 1.5
- gate_weight: bfloat16 [4096, 14336], P(None, 'tp'), may hold values from -0.09375 to 0.09375
- up_weight: bfloat16 [4096, 14336], P(None, 'tp'), may hold values from -0.09375 to 0.09375
- down_weight: bfloat16 [14336, 4096], P('tp'), may hold values from -0.046875 to 0.046875
- cotangent: bfloat16 [4096, 4096], P(('dp', 'tp')), may hold values from -4 to 4
Outputs:
- mixed: bfloat16 [4096, 4096], P(('dp', 'tp'))
- token_gradient: bfloat16 [4096, 4096], P(('dp', 'tp'))
- grad_gate: bfloat16 [4096, 14336], P('dp', 'tp')
- grad_up: bfloat16 [4096, 14336], P('dp', 'tp')
- grad_down: bfloat16 [14336, 4096], P('tp', 'dp')
All inputs are finite; a program needn't handle non-finite values.
Results may differ from a plain program's by a relative error of at most 0.025.
Values may be sent and summed in bfloat16 or wider, within the bound.
A program may use at most 128 MiB of HBM per device.

v0:
```python
import jax
import jax.numpy as jnp
from jax import lax
from jax.sharding import PartitionSpec as P


def contract_rows(left, right):
    return lax.dot_general(
        left, right, (((0,), (0,)), ((), ())), preferred_element_type=jnp.float32
    )


def contract_cols(left, right):
    return lax.dot_general(
        left, right, (((1,), (1,)), ((), ())), preferred_element_type=jnp.float32
    )


def local(tokens, norm_scale_vector, gate_weight, up_weight, down_weight, cotangent):
    expanded_hidden = tokens.astype(jnp.float32)
    reciprocal_root_mean = lax.rsqrt(
        jnp.mean(expanded_hidden * expanded_hidden, axis=-1, keepdims=True) + 1e-05
    )
    unit_input = expanded_hidden * reciprocal_root_mean
    rescaled_input = (unit_input * norm_scale_vector).astype(jnp.bfloat16)
    normed_all = lax.all_gather(rescaled_input, "tp", axis=0, tiled=True)
    gate = jnp.dot(normed_all, gate_weight, preferred_element_type=jnp.float32)
    lifted = jnp.dot(normed_all, up_weight, preferred_element_type=jnp.float32)
    sigmoid_gate = jax.nn.sigmoid(gate)
    activated = gate * sigmoid_gate
    hidden = (activated * lifted).astype(jnp.bfloat16)
    branch = lax.psum_scatter(
        jnp.dot(hidden, down_weight, preferred_element_type=jnp.float32).astype(jnp.bfloat16),
        "tp",
        scatter_dimension=0,
        tiled=True,
    ).astype(jnp.float32)
    mixed = (expanded_hidden + branch).astype(jnp.bfloat16)
    grad_all = lax.all_gather(cotangent, "tp", axis=0, tiled=True)
    grad_hidden = contract_cols(grad_all, down_weight)
    grad_pre = (grad_hidden * lifted * sigmoid_gate * (1.0 + gate * (1.0 - sigmoid_gate))).astype(
        jnp.bfloat16
    )
    grad_lifted = (grad_hidden * activated).astype(jnp.bfloat16)
    grad_normed = lax.psum_scatter(
        (contract_cols(grad_pre, gate_weight) + contract_cols(grad_lifted, up_weight)).astype(
            jnp.bfloat16
        ),
        "tp",
        scatter_dimension=0,
        tiled=True,
    ).astype(jnp.float32)
    gain_applied = grad_normed * norm_scale_vector
    inner_product = jnp.mean(gain_applied * unit_input, axis=-1, keepdims=True)
    token_gradient = (
        cotangent.astype(jnp.float32)
        + reciprocal_root_mean * (gain_applied - unit_input * inner_product)
    ).astype(jnp.bfloat16)
    weight_gate = contract_rows(normed_all, grad_pre).astype(jnp.bfloat16)
    weight_up = contract_rows(normed_all, grad_lifted).astype(jnp.bfloat16)
    weight_down = contract_rows(hidden, grad_all).astype(jnp.bfloat16)
    sum_gate, sum_up, sum_down = (
        lax.psum_scatter(weight_gate, "dp", scatter_dimension=0, tiled=True).astype(jnp.float32),
        lax.psum_scatter(weight_up, "dp", scatter_dimension=0, tiled=True).astype(jnp.float32),
        lax.psum_scatter(weight_down, "dp", scatter_dimension=1, tiled=True).astype(jnp.float32),
    )
    return (
        mixed,
        token_gradient,
        sum_gate.astype(jnp.bfloat16),
        sum_up.astype(jnp.bfloat16),
        sum_down.astype(jnp.bfloat16),
    )


def solution(mesh):
    in_specs = (
        P(("dp", "tp"), None),
        P(),
        P(None, "tp"),
        P(None, "tp"),
        P("tp", None),
        P(("dp", "tp"), None),
    )
    out_specs = (
        P(("dp", "tp"), None),
        P(("dp", "tp"), None),
        P("dp", "tp"),
        P("dp", "tp"),
        P("tp", "dp"),
    )
    return jax.shard_map(local, mesh=mesh, in_specs=in_specs, out_specs=out_specs, check_vma=False)
```

profile of v0, /device:TPU:1, one launch (start us, length us, event | category | flops | bytes accessed | tf_op | source)
XLA Modules:
  0.0 686.7 jit_solution(14147449876806894025)
XLA Ops:
  7.2 0.0 all-gather.3.cloned.1.call-start
  7.2 1.1 fusion.10
  8.3 1.7 fusion.4
  9.9 0.0 all-gather.3.cloned.1.call-update
  10.0 0.0 all-gather.5.cloned.1.call-start
  10.0 0.7 all-gather.5.cloned.1.call-update
  10.7 0.0 reduce-scatter.8.cloned.1.call-start
  10.8 70.7 %all-gather.3.cloned.1.call-done = bf16[512,4096]{1,0:T(8,128)(2,1)} async-done(((bf16[16,4096]{1,0:T(8,128)(2,1)}), bf16[512,4096]{1,0:T(8,128)(2,1)}) %all-gather.3.cloned.1.call-update) | async-done | bytes 4194320 | tf_op jit(solution)/shard_map/all_gather | solution.py:26
  81.5 0.0 copy-start
  81.5 0.0 copy-start.6
  81.5 5.5 fusion.13
  87.0 0.0 copy-done
  87.1 0.1 copy-done.6
  87.1 2.1 fusion.12
  89.2 60.6 %all-gather.5.cloned.1.call-done = bf16[512,4096]{1,0:T(8,128)(2,1)} async-done(((bf16[16,4096]{1,0:T(8,128)(2,1)}), bf16[512,4096]{1,0:T(8,128)(2,1)}) %all-gather.5.cloned.1.call-update) | async-done | bytes 4194320 | tf_op jit(solution)/shard_map/all_gather | solution.py:39
  149.8 0.0 copy-start.1
  149.8 5.9 multiply_convert_fusion
  155.7 0.0 copy-done.1
  155.7 0.0 copy-start.2
  155.7 2.4 fusion.14
  158.2 0.0 copy-done.2
  158.2 4.6 add_convert_fusion
  162.8 0.0 reduce-scatter.8.cloned.1.call-update
  162.8 0.2 reduce-scatter.6.cloned.1.call-start
  163.1 6.4 convolution_convert_fusion
  169.4 0.0 reduce-scatter.6.cloned.1.call-update
  169.4 0.0 reduce-scatter.14.cloned.1.call-start
  169.5 6.1 convolution_convert_fusion.3
  175.6 0.0 reduce-scatter.14.cloned.1.call-update
  175.6 0.0 reduce-scatter.10.cloned.1.call-start
  175.6 6.1 convolution_convert_fusion.2
  181.7 0.0 reduce-scatter.10.cloned.1.call-update
  181.7 0.0 copy-start.3
  181.7 0.0 copy-start.5
  181.8 0.0 copy-start.4
  181.8 0.0 reduce-scatter.12.cloned.1.call-start
  181.8 6.2 convolution_convert_fusion.1
  188.1 0.0 reduce-scatter.12.cloned.1.call-update
  188.1 93.3 %reduce-scatter.8.cloned.1.call-done = bf16[16,4096]{1,0:T(8,128)(2,1)} async-done(((bf16[512,4096]{1,0:T(8,128)(2,1)}), bf16[16,4096]{1,0:T(8,128)(2,1)}) %reduce-scatter.8.cloned.1.call-update) | async-done | bytes 131088 | tf_op jit(solution)/shard_map/reduce_scatter | solution.py:45
  281.4 0.0 copy-done.3
  281.4 0.0 copy-done.5
  281.4 1.1 fusion.5
  282.5 122.6 %reduce-scatter.6.cloned.1.call-done = bf16[16,4096]{1,0:T(8,128)(2,1)} async-done(((bf16[512,4096]{1,0:T(8,128)(2,1)}), bf16[16,4096]{1,0:T(8,128)(2,1)}) %reduce-scatter.6.cloned.1.call-update) | async-done | bytes 131088 | tf_op jit(solution)/shard_map/reduce_scatter | solution.py:32
  405.2 0.0 copy-done.4
  405.2 1.8 fusion.9
  406.9 90.5 %reduce-scatter.14.cloned.1.call-done = bf16[448,512]{1,0:T(8,128)(2,1)} async-done(((bf16[448,4096]{1,0:T(8,128)(2,1)}), bf16[448,512]{1,0:T(8,128)(2,1)}) %reduce-scatter.14.cloned.1.call-update) | async-done | bytes 458768 | tf_op jit(solution)/shard_map/reduce_scatter | solution.py:65
  497.5 91.5 %reduce-scatter.10.cloned.1.call-done = bf16[512,448]{0,1:T(8,128)(2,1)} async-done(((bf16[4096,448]{0,1:T(8,128)(2,1)}), bf16[512,448]{0,1:T(8,128)(2,1)}) %reduce-scatter.10.cloned.1.call-update) | async-done | bytes 458768 | tf_op jit(solution)/shard_map/reduce_scatter | solution.py:63
  588.9 91.0 %reduce-scatter.12.cloned.1.call-done = bf16[512,448]{0,1:T(8,128)(2,1)} async-done(((bf16[4096,448]{0,1:T(8,128)(2,1)}), bf16[512,448]{0,1:T(8,128)(2,1)}) %reduce-scatter.12.cloned.1.call-update) | async-done | bytes 458768 | tf_op jit(solution)/shard_map/reduce_scatter | solution.py:64
  (2 shorter events, 0.0 us)
Async XLA Ops:
  7.2 74.3 %all-gather.3.cloned.1.call-start = ((), (), s32[]{:S(2)}) async-start(), calls=%async_computation.5 | async-start | bytes 4325376 | tf_op jit(solution)/shard_map/all_gather | solution.py:26
  10.0 139.9 %all-gather.5.cloned.1.call-start = ((), (), s32[]{:S(2)}) async-start(), calls=%async_computation.7 | async-start | bytes 4325376 | tf_op jit(solution)/shard_map/all_gather | solution.py:39
  10.7 270.7 %reduce-scatter.8.cloned.1.call-start = ((), (), s32[]{:S(2)}) async-start(), calls=%async_computation.8 | async-start | bytes 4325376 | tf_op jit(solution)/shard_map/reduce_scatter | solution.py:45
  81.5 5.6 copy-start
  81.5 5.6 copy-start.6
  149.8 5.9 copy-start.1
  155.7 2.4 copy-start.2
  162.8 242.4 %reduce-scatter.6.cloned.1.call-start = ((), (), s32[]{:S(2)}) async-start(), calls=%async_computation.6 | async-start | bytes 4325376 | tf_op jit(solution)/shard_map/reduce_scatter | solution.py:32
  169.4 328.0 %reduce-scatter.14.cloned.1.call-start = ((), (), s32[]{:S(2)}) async-start(), calls=%async_computation.11 | async-start | bytes 4128768 | tf_op jit(solution)/shard_map/reduce_scatter | solution.py:65
  175.6 413.4 %reduce-scatter.10.cloned.1.call-start = ((), (), s32[]{:S(2)}) async-start(), calls=%async_computation.9 | async-start | bytes 4128768 | tf_op jit(solution)/shard_map/reduce_scatter | solution.py:63
  181.7 99.7 %copy-start.3 = (bf16[16,4096]{1,0:T(8,128)(2,1)S(1)}, bf16[16,4096]{1,0:T(8,128)(2,1)}, u32[]{:S(2)}) copy-start(bf16[16,4096]{1,0:T(8,128)(2,1)} %param.6) | copy-start | bytes 393220
  181.7 99.7 %copy-start.5 = (f32[4096]{0:T(1024)S(1)}, f32[4096]{0:T(1024)}, u32[]{:S(2)}) copy-start(f32[4096]{0:T(1024)} %param.7) | copy-start | bytes 49156
  181.8 223.4 %copy-start.4 = (bf16[16,4096]{1,0:T(8,128)(2,1)S(1)}, bf16[16,4096]{1,0:T(8,128)(2,1)}, u32[]{:S(2)}) copy-start(bf16[16,4096]{1,0:T(8,128)(2,1)} %param.11) | copy-start | bytes 393220
  181.8 498.1 %reduce-scatter.12.cloned.1.call-start = ((), (), s32[]{:S(2)}) async-start(), calls=%async_computation.10 | async-start | bytes 4128768 | tf_op jit(solution)/shard_map/reduce_scatter | solution.py:64
Sparse Core Ops, SparseCore 0:
  10.4 71.0 all-gather.2
  83.3 66.4 all-gather.4
  162.9 118.4 reduce-scatter.7
  283.8 121.3 reduce-scatter.5
  409.9 87.5 reduce-scatter.13
  502.7 86.1 reduce-scatter.9
  593.8 86.0 reduce-scatter.11
where the time goes:
time: 687 us
  waiting for transfers between devices  621 us (90%)
  matrix products  45.3 us (7%)
  between operations  14.2 us (2%)
    reduce_scatter x1, waiting for transfers between devices, local(): lax.psum_scatter(jnp.dot(hidden, down_weight, preferred_element_type=jnp....  123 us
    reduce_scatter x1, waiting for transfers between devices, local(): lax.psum_scatter((contract_cols(grad_pre, gate_weight) + contract_cols(gr...  93.3 us
    reduce_scatter x1, waiting for transfers between devices, local(): lax.psum_scatter(weight_gate, 'dp', scatter_dimension=0, tiled=True)  91.5 us
    reduce_scatter x1, waiting for transfers between devices, local(): lax.psum_scatter(weight_up, 'dp', scatter_dimension=0, tiled=True)  91 us
    reduce_scatter x1, waiting for transfers between devices, local(): lax.psum_scatter(weight_down, 'dp', scatter_dimension=1, tiled=True)  90.5 us
    all_gather x1, waiting for transfers between devices, local(): normed_all = lax.all_gather(rescaled_input, 'tp', axis=0, tiled=True)  70.7 us
    all_gather x1, waiting for transfers between devices, local(): grad_all = lax.all_gather(cotangent, 'tp', axis=0, tiled=True)  60.6 us
    dot_general x3, matrix products, contract_rows(): lax.dot_general(left, right, (((0,), (0,)), ((), ())), preferred_element_...  18.4 us
  transfers between devices with their start and end apart: 7, of which 7 were waited for; matrix products, arithmetic and copies ran while one was open for 5% of the time, Pallas kernels for 0%

commit v1 on v0

v1 whole, which is shorter than its diff:
```python
import functools

import jax
import jax.numpy as jnp
from jax import lax
from jax.experimental import pallas as pl
from jax.experimental.pallas import tpu as pltpu
from jax.sharding import PartitionSpec as P

BF16 = jnp.bfloat16
F32 = jnp.float32
MESH = pl.DeviceIdType.MESH
D = 4096
W = 448
ROWS = 16
NZ = 8
SPLIT = 2048
HALF = 2048
CH = 512
TILE = 512


def kernel(
    tok, scale, cot, gw, uw, dw,
    mixed, tgrad, wout,
    nrm, ctg, ext, wg, wu, wd, acc, hid, gpr, glf, tra, part, crecv, zrecv, yst, yrecv,
    wch, xr1, xr2, lsem, ssem, rsem,
):
    d, t = lax.axis_index("dp"), lax.axis_index("tp")
    yh, x = d // 4, d % 4
    z, yl, c = t // 4, (t // 2) % 2, t % 2
    zdev = {s: (d, ((z + s + NZ) % NZ) * 4 + yl * 2 + c) for s in (1, -1)}
    ydev = (d, z * 4 + (1 - yl) * 2 + c)
    cdev = (d, z * 4 + yl * 2 + (1 - c))
    xdev = {s: (yh * 4 + (x + s + 4) % 4, t) for s in (1, -1)}
    hdev = ((1 - yh) * 4 + x, t)
    partners = [zdev[1], zdev[-1], ydev, cdev, xdev[1], xdev[-1], hdev]

    loads = [
        pltpu.make_async_copy(src, dst, lsem.at[i])
        for i, (src, dst) in enumerate(((gw, wg), (uw, wu), (dw, wd)))
    ]
    for load in loads:
        load.start()

    sent = []

    def send(src, dst, device):
        at = len(sent)
        copy = pltpu.make_async_remote_copy(
            src_ref=src, dst_ref=dst, send_sem=ssem.at[at], recv_sem=rsem.at[at],
            device_id=device, device_id_type=MESH,
        )
        copy.start()
        sent.append(copy)
        return copy

    def normalized():
        xf = tok[...].astype(F32)
        r = lax.rsqrt(jnp.mean(xf * xf, axis=-1, keepdims=True) + 1e-05)
        return xf, r, xf * r

    nrm[z, yl, c] = (normalized()[2] * scale[...]).astype(BF16)
    ctg[z, yl, c] = cot[...]

    barrier = pltpu.get_barrier_semaphore()
    for device in partners:
        pl.semaphore_signal(barrier, inc=1, device_id=device, device_id_type=MESH)
    pl.semaphore_wait(barrier, len(partners))

    def gather(buf):
        def cols(lo, hi, h, s):
            if h < 4:
                return pl.ds(lo, hi - lo)
            mid = (lo + hi) // 2
            return pl.ds(lo, mid - lo) if s == 1 else pl.ds(mid, hi - mid)

        def a_slab(zz, h, s):
            return buf.at[zz, yl, c, :, cols(0, SPLIT, h, s)]

        def b_slab(zz, h, s):
            return buf.at[zz, pl.ds(0, 2), c, :, cols(SPLIT, D, h, s)]

        own_b = buf.at[z, yl, c, :, pl.ds(SPLIT, D - SPLIT)]
        yb = send(own_b, own_b, ydev)
        za, zb = {}, {}
        for s in (1, -1):
            za[s] = send(a_slab(z, 1, s), a_slab(z, 1, s), zdev[s])
        ya = send(a_slab(z, 1, 1), a_slab(z, 1, 1), ydev)
        yield
        yb.wait_recv()
        for s in (1, -1):
            zb[s] = send(b_slab(z, 1, s), b_slab(z, 1, s), zdev[s])
        yield
        pending, core = [(z, [ya])], []

        def flush():
            for zz, arrivals in pending:
                for arrival in arrivals:
                    arrival.wait_recv()
                both = buf.at[zz, pl.ds(0, 2), c]
                core.append(send(both, both, cdev))

        for h in (1, 2, 3, 4):
            fresh = []
            for s in (1, -1):
                zz = (z - s * h + NZ) % NZ
                za[s].wait_recv()
                if h < 4:
                    za[s] = send(a_slab(zz, h + 1, s), a_slab(zz, h + 1, s), zdev[s])
                yf = send(a_slab(zz, h, s), a_slab(zz, h, s), ydev)
                zb[s].wait_recv()
                if h < 4:
                    zb[s] = send(b_slab(zz, h + 1, s), b_slab(zz, h + 1, s), zdev[s])
                if h == 4 and s == -1:
                    fresh[0][1].append(yf)
                else:
                    fresh.append((zz, [yf]))
            yield
            flush()
            pending = fresh
            yield
        flush()
        for copy in core:
            copy.wait_recv()

    def run(*gens):
        live = list(gens)
        while live:
            for g in list(live):
                if next(g, 1) == 1:
                    live.remove(g)

    half = pl.ds(pl.multiple_of((1 - yh) * HALF, HALF), HALF)
    seeds = [
        send(src.at[z, yl, c, :, half], ext.at[z, yl, c, :, pl.ds(i * HALF, HALF)], hdev)
        for i, src in enumerate((nrm, ctg))
    ]
    run(gather(nrm), gather(ctg))

    def seeded():
        for seed in seeds:
            seed.wait_recv()
        yield from gather(ext)

    third = seeded()

    def tokens_of(buf, col, width):
        return buf[:, :, :, :, pl.ds(col, width)].reshape(NZ * 4 * ROWS, width)

    for load in loads:
        load.wait()

    next(third, None)
    acc[...] = jnp.zeros_like(acc)

    def into(i, buf, weight):
        @pl.loop(0, D // TILE)
        def _(k):
            at = pl.multiple_of(k * TILE, TILE)
            acc[i] += jnp.dot(
                tokens_of(buf, at, TILE), weight[pl.ds(at, TILE), :],
                preferred_element_type=F32,
            )

    into(0, nrm, wg)
    next(third, None)
    into(1, nrm, wu)
    next(third, None)

    @pl.loop(0, D // TILE)
    def _(k):
        at = pl.multiple_of(k * TILE, TILE)
        acc[2] += lax.dot_general(
            tokens_of(ctg, at, TILE), wd[:, pl.ds(at, TILE)], (((1,), (1,)), ((), ())),
            preferred_element_type=F32,
        )

    next(third, None)

    @pl.loop(0, 4)
    def _(k):
        rows = pl.ds(pl.multiple_of(k * 128, 128), 128)
        gate, lifted, gh = acc[0, rows, :], acc[1, rows, :], acc[2, rows, :]
        sg = jax.nn.sigmoid(gate)
        act = gate * sg
        h = act * lifted
        gp = gh * lifted * sg * (1.0 + gate * (1.0 - sg))
        gl = gh * act
        hid[rows, :] = h.astype(BF16)
        gpr[rows, :] = gp.astype(BF16)
        glf[rows, :] = gl.astype(BF16)
        tra[0, pl.ds(0, W), rows] = h.T.astype(BF16)
        tra[0, pl.ds(W, W), rows] = gp.T.astype(BF16)
        tra[0, pl.ds(2 * W, W), rows] = gl.T.astype(BF16)

    swaps = []
    for g in range(3):
        rows = pl.ds(g * W, W)
        swaps.append(send(tra.at[0, rows], tra.at[1, rows], hdev))

    next(third, None)

    @pl.loop(0, D // TILE)
    def _(k):
        at = pl.multiple_of(k * TILE, TILE)
        out = jnp.dot(hid[...], wd[:, pl.ds(at, TILE)], preferred_element_type=F32)
        part[0, :, :, :, :, pl.ds(at, TILE)] = out.astype(BF16).reshape(NZ, 2, 2, ROWS, TILE)

    def scatter(i):
        theirs = part.at[i, pl.ds(0, NZ), pl.ds(0, 2), 1 - c]
        core = send(theirs, crecv.at[i], cdev)
        yield
        core.wait_recv()
        arrived = {}
        for h in range(4):
            for s in (1, -1):
                zz = (z + s * (4 - h) + NZ) % NZ
                if h == 0:
                    cols = pl.ds(0, D // 2) if s == 1 else pl.ds(D // 2, D // 2)
                    total = part[i, zz, :, c, :, cols].astype(F32) + crecv[i, zz, :, :, cols].astype(F32)
                    part[i, zz, :, c, :, cols] = total.astype(BF16)
                else:
                    arrived[s].wait_recv()
                    for cols, added in (
                        (pl.ds(0, D // 2), h > 1 or s == 1),
                        (pl.ds(D // 2, D // 2), h > 1 or s == -1),
                    ):
                        total = part[i, zz, :, c, :, cols].astype(F32) + crecv[i, zz, :, :, cols].astype(F32)
                        if added:
                            total = total + zrecv[i, s2(s), h - 1, :, :, cols].astype(F32)
                        part[i, zz, :, c, :, cols] = total.astype(BF16)
                    cols = pl.ds(0, D)
                arrived[s] = send(
                    part.at[i, zz, pl.ds(0, 2), c, :, cols],
                    zrecv.at[i, s2(s), h, pl.ds(0, 2), :, cols],
                    zdev[s],
                )
            yield
        for s in (1, -1):
            arrived[s].wait_recv()

        def total_of(y):
            return (
                part[i, z, y, c].astype(F32) + crecv[i, z, y].astype(F32)
                + zrecv[i, 0, 3, y].astype(F32) + zrecv[i, 1, 3, y].astype(F32)
            )

        yst[i] = total_of(1 - yl).astype(BF16)
        last = send(yst.at[i], yrecv.at[i], ydev)
        yield
        last.wait_recv()
        total = total_of(yl) + yrecv[i].astype(F32)
        xf, r, unit = normalized()
        if i == 0:
            mixed[...] = (xf + total).astype(BF16)
        else:
            gain = total * scale[...]
            inner = jnp.mean(gain * unit, axis=-1, keepdims=True)
            tgrad[...] = (cot[...].astype(F32) + r * (gain - unit * inner)).astype(BF16)

    def s2(s):
        return 0 if s == 1 else 1

    forward = scatter(0)
    next(forward)
    next(third, None)

    @pl.loop(0, D // TILE)
    def _(k):
        at = pl.multiple_of(k * TILE, TILE)
        dims = (((1,), (1,)), ((), ()))
        out = lax.dot_general(gpr[...], wg[pl.ds(at, TILE), :], dims, preferred_element_type=F32)
        out += lax.dot_general(glf[...], wu[pl.ds(at, TILE), :], dims, preferred_element_type=F32)
        part[1, :, :, :, :, pl.ds(at, TILE)] = out.astype(BF16).reshape(NZ, 2, 2, ROWS, TILE)

    backward = scatter(1)
    next(backward)
    next(forward)
    run(third)
    next(backward)

    q = W // 2

    def weights(g, xx):
        rows = pl.ds(g * W, W)
        own = ctg if g == 0 else nrm
        at = pl.multiple_of(yh * HALF + xx * CH, CH)
        far = pl.multiple_of((HALF if g == 0 else 0) + xx * CH, CH)
        out = jnp.dot(tra[0, rows, :], tokens_of(own, at, CH), preferred_element_type=F32)
        out += jnp.dot(tra[1, rows, :], tokens_of(ext, far, CH), preferred_element_type=F32)
        return out

    def over_x(g):
        up, down = pl.ds(g * W, q), pl.ds(g * W + q, q)
        rows = pl.ds(g * W, W)
        swaps[g].wait_recv()
        far = (x + 2) % 4
        wch[0, rows, :] = weights(g, far).astype(BF16)
        one = send(wch.at[0, up], xr1.at[0, pl.ds(g * q, q)], xdev[1])
        two = send(wch.at[0, down], xr1.at[1, pl.ds(g * q, q)], xdev[-1])
        wch[1, rows, :] = weights(g, (x + 1) % 4).astype(BF16)
        three = send(wch.at[1, down], xr2.at[0, down], xdev[1])
        wch[2, rows, :] = weights(g, (x + 3) % 4).astype(BF16)
        four = send(wch.at[2, up], xr2.at[1, up], xdev[-1])
        yield
        one.wait_recv()
        wch[1, up, :] = (wch[1, up, :].astype(F32) + xr1[0, pl.ds(g * q, q)].astype(F32)).astype(BF16)
        five = send(wch.at[1, up], xr2.at[0, up], xdev[1])
        two.wait_recv()
        wch[2, down, :] = (wch[2, down, :].astype(F32) + xr1[1, pl.ds(g * q, q)].astype(F32)).astype(BF16)
        six = send(wch.at[2, down], xr2.at[1, down], xdev[-1])
        yield
        mine = weights(g, x)
        for copy in (three, four, five, six):
            copy.wait_recv()
        wout[rows, :] = (mine + xr2[0, rows].astype(F32) + xr2[1, rows].astype(F32)).astype(BF16)

    thirds = [over_x(g) for g in range(3)]
    next(thirds[0])
    next(forward)
    next(backward)
    next(thirds[0])
    next(thirds[1])
    next(forward)
    next(backward)
    next(thirds[1])
    next(thirds[2])
    next(forward)
    next(backward)
    run(thirds[0])
    next(thirds[2])
    next(forward)
    next(backward)
    run(thirds[1])
    run(forward)
    run(backward)
    run(thirds[2])

    for copy in sent:
        copy.wait_send()


def local(tokens, norm_scale_vector, gate_weight, up_weight, down_weight, cotangent):
    vmem = pl.BlockSpec(memory_space=pltpu.VMEM)
    hbm = pl.BlockSpec(memory_space=pl.ANY)
    slab = (NZ, 2, 2, ROWS, D)
    count = 192
    mixed, tgrad, wout = pl.pallas_call(
        kernel,
        out_shape=(
            jax.ShapeDtypeStruct((ROWS, D), BF16),
            jax.ShapeDtypeStruct((ROWS, D), BF16),
            jax.ShapeDtypeStruct((3 * W, CH), BF16),
        ),
        in_specs=[vmem, vmem, vmem, hbm, hbm, hbm],
        out_specs=(vmem, vmem, vmem),
        scratch_shapes=[
            pltpu.VMEM(slab, BF16),
            pltpu.VMEM(slab, BF16),
            pltpu.VMEM(slab, BF16),
            pltpu.VMEM((D, W), BF16),
            pltpu.VMEM((D, W), BF16),
            pltpu.VMEM((W, D), BF16),
            pltpu.VMEM((3, 512, W), F32),
            pltpu.VMEM((512, W), BF16),
            pltpu.VMEM((512, W), BF16),
            pltpu.VMEM((512, W), BF16),
            pltpu.VMEM((2, 3 * W, 512), BF16),
            pltpu.VMEM((2, *slab), BF16),
            pltpu.VMEM((2, NZ, 2, ROWS, D), BF16),
            pltpu.VMEM((2, 2, 4, 2, ROWS, D), BF16),
            pltpu.VMEM((2, ROWS, D), BF16),
            pltpu.VMEM((2, ROWS, D), BF16),
            pltpu.VMEM((3, 3 * W, CH), BF16),
            pltpu.VMEM((2, 3 * W // 2, CH), BF16),
            pltpu.VMEM((2, 3 * W, CH), BF16),
            pltpu.SemaphoreType.DMA((3,)),
            pltpu.SemaphoreType.DMA((count,)),
            pltpu.SemaphoreType.DMA((count,)),
        ],
        compiler_params=pltpu.CompilerParams(
            collective_id=0, has_side_effects=True, vmem_limit_bytes=62 << 20
        ),
        cost_estimate=pl.CostEstimate(
            flops=2 * 9 * 512 * D * W, bytes_accessed=16 << 20, transcendentals=512 * W
        ),
        name="ffn",
    )(tokens, norm_scale_vector.reshape(1, D), cotangent, gate_weight, up_weight, down_weight)
    return mixed, tgrad, wout[W : 2 * W].T, wout[2 * W :].T, wout[:W]


def solution(mesh):
    both, rows = P(("dp", "tp"), None), P()
    return jax.shard_map(
        local,
        mesh=mesh,
        in_specs=(both, rows, P(None, "tp"), P(None, "tp"), P("tp", None), both),
        out_specs=(both, both, P("dp", "tp"), P("dp", "tp"), P("tp", "dp")),
        check_vma=False,
    )
```

time: 687 us -> 175 us (0.25)
  waiting for transfers between devices: 621 us -> 0 us
  Pallas kernels: 0 us -> 156 us
  matrix products: 45.3 us -> 0 us
  local copies, waits for them, and re-layouts: 0.09 us -> 18.4 us
  between operations: 14.2 us -> 0.64 us
    reduce_scatter x5 -> x0, waiting for transfers between devices: 489 us -> none  [the longest x1 123 us: local(): lax.psum_scatter(jnp.dot(hidden, down_weight, preferred_element_type=jnp....]
    pallas_call x0 -> x1, Pallas kernels: none -> 156 us  [local(): pl.pallas_call(kernel, out_shape=(jax.ShapeDtypeStruct((ROWS, D), BF16),...]
    all_gather x2 -> x0, waiting for transfers between devices: 131 us -> none  [the longest x1 70.7 us: local(): normed_all = lax.all_gather(rescaled_input, 'tp', axis=0, tiled=True)]
    dot_general x9 -> x0, matrix products: 45.3 us -> none  [the longest x3 18.4 us: contract_rows(): lax.dot_general(left, right, (((0,), (0,)), ((), ())), preferred_element_...]
    unnamed x14 -> x4, local copies, waits for them, and re-layouts: 0.09 us -> 16 us
  transfers between devices with their start and end apart: 7 -> 0, of which waited for: 7 -> 0; matrix products, arithmetic and copies ran while one was open for 5% -> 0% of each run, Pallas kernels for 0% -> 0%
where the time goes in v1:
time: 175 us
  Pallas kernels  156 us (89%)
  local copies, waits for them, and re-layouts  18.4 us (11%)
    pallas_call x1, Pallas kernels, local(): pl.pallas_call(kernel, out_shape=(jax.ShapeDtypeStruct((ROWS, D), BF16),...  156 us
    unnamed x4, local copies, waits for them, and re-layouts  16 us

profile of v1, /device:TPU:1, one launch (start us, length us, event | category | flops | bytes accessed | tf_op | source)
XLA Modules:
  0.0 175.1 jit_solution(11805697582851926038)
XLA Ops:
  0.6 6.4 %copy.11.gw = bf16[4096,448]{1,0:T(8,128)(2,1)} copy(bf16[4096,448]{0,1:T(8,128)(2,1)} %param.8) | data formatting | bytes 7340032 | tf_op args[2]
  7.0 6.5 %copy.12.uw = bf16[4096,448]{1,0:T(8,128)(2,1)} copy(bf16[4096,448]{0,1:T(8,128)(2,1)} %param.9) | data formatting | bytes 7340032 | tf_op args[3]
  13.5 156.0 %ffn.1 = (bf16[16,4096]{1,0:T(8,128)(2,1)}, bf16[16,4096]{1,0:T(8,128)(2,1)}, bf16[1344,512]{1,0:T(8,128)(2,1)}) custom-call(bf16[16,4096]{1,0:T(8,128)(2,1)} %tok.1, f32[1,4096]{1,0:T(1,128)} %bitcast.5, bf16[16,4096]{1,0:T(8,128)(2,1)} %cot.1, bf16[4096,448]{1,0:T(8,128)(2,1)} %copy.11.gw, bf16[4096,448]{1,0:T(8,128)(2,1)} %copy.12.uw, bf16[448,4096]{1,0:T(8,128)(2,1)} %dw.1), custom_call_target="tpu_custom_call" | custom-call | flops 16911433728 | bytes 16777216 | tf_op jit(solution)/shard_map/ffn/pallas_call | solution.py:349
  169.5 2.4 %fusion = (bf16[448,512]{1,0:T(8,128)(2,1)}, bf16[512,448]{0,1:T(8,128)(2,1)}, bf16[512,448]{0,1:T(8,128)(2,1)}) fusion(bf16[1344,512]{1,0:T(8,128)(2,1)} %get-tuple-element.10), kind=kLoop, calls=%fused_computation.2 | loop fusion | bytes 2752512 | tf_op jit(solution)/shard_map/slice | solution.py:390
  171.9 1.6 copy.15
  173.5 1.6 copy.16

commit v2 on v1

v2 whole, which is shorter than its diff:
```python
import functools

import jax
import jax.numpy as jnp
from jax import lax
from jax.experimental import pallas as pl
from jax.experimental.pallas import tpu as pltpu
from jax.sharding import PartitionSpec as P

BF16 = jnp.bfloat16
F32 = jnp.float32
MESH = pl.DeviceIdType.MESH
D = 4096
W = 448
ROWS = 16
NZ = 8
HALF = 2048
CH = 512
TILE = 512


def kernel(
    tok, scale, cot, gw, uw, dw,
    mixed, tgrad, wout,
    nrm, ctg, ext, wg, wu, wd, acc, hid, gpr, glf, tra, got, part, crecv, zrecv, yst, yrecv,
    vch, vr1, vr2, vst, vrecv, wch, xr1, xr2, lsem, ssem, rsem,
):
    d, t = lax.axis_index("dp"), lax.axis_index("tp")
    yh, x = d // 4, d % 4
    z, yl, c = t // 4, (t // 2) % 2, t % 2
    zdev = {s: (d, ((z + s + NZ) % NZ) * 4 + yl * 2 + c) for s in (1, -1)}
    ydev = (d, z * 4 + (1 - yl) * 2 + c)
    cdev = (d, z * 4 + yl * 2 + (1 - c))
    xdev = {s: (yh * 4 + (x + s + 4) % 4, t) for s in (1, -1)}
    hdev = ((1 - yh) * 4 + x, t)
    partners = [zdev[1], zdev[-1], ydev, cdev, xdev[1], xdev[-1], hdev]

    barrier = pltpu.get_barrier_semaphore()
    for device in partners:
        pl.semaphore_signal(barrier, inc=1, device_id=device, device_id_type=MESH)

    loads = [
        pltpu.make_async_copy(src, dst, lsem.at[i])
        for i, (src, dst) in enumerate(((gw, wg), (uw, wu), (dw, wd)))
    ]
    for load in loads:
        load.start()

    sent = []

    def send(src, dst, device):
        at = len(sent)
        copy = pltpu.make_async_remote_copy(
            src_ref=src, dst_ref=dst, send_sem=ssem.at[at], recv_sem=rsem.at[at],
            device_id=device, device_id_type=MESH,
        )
        copy.start()
        sent.append(copy)
        return copy

    def normalized():
        xf = tok[...].astype(F32)
        r = lax.rsqrt(jnp.mean(xf * xf, axis=-1, keepdims=True) + 1e-05)
        return xf, r, xf * r

    nrm[z, yl, c] = (normalized()[2] * scale[...]).astype(BF16)
    ctg[z, yl, c] = cot[...]
    pl.semaphore_wait(barrier, len(partners))

    def gather(buf, width):
        def one(zz, y, s=0):
            mid = width // 2
            cols = {0: pl.ds(0, width), 1: pl.ds(0, mid), -1: pl.ds(mid, mid)}[s]
            return buf.at[zz, y, c, :, cols]

        def both(zz, s=0):
            mid = width // 2
            cols = {0: pl.ds(0, width), 1: pl.ds(0, mid), -1: pl.ds(mid, mid)}[s]
            return buf.at[zz, pl.ds(0, 2), c, :, cols]

        def push(ref, device):
            return send(ref, ref, device)

        at = {(s, h): (z - s * h + NZ) % NZ for s in (1, -1) for h in (1, 2, 3, 4)}
        ways = (1, -1)
        z1 = {s: push(one(z, yl), zdev[s]) for s in ways}
        y0 = push(one(z, yl), ydev)
        yield
        z2, y1 = {}, {}
        for s in ways:
            z1[s].wait_recv()
            z2[s] = push(one(at[s, 1], yl), zdev[s])
            y1[s] = push(one(at[s, 1], yl), ydev)
        yield
        y0.wait_recv()
        core = [push(both(z), cdev)]
        z3, y2, z3b = {}, {}, {}
        for s in ways:
            z2[s].wait_recv()
            z3[s] = push(one(at[s, 2], yl), zdev[s])
            y2[s] = push(one(at[s, 2], yl), ydev)
        yield
        for s in ways:
            y1[s].wait_recv()
            core.append(push(both(at[s, 1]), cdev))
        for s in ways:
            y2[s].wait_recv()
            z3b[s] = push(one(at[s, 2], 1 - yl), zdev[s])
        yield
        z4, z4b = {}, {}
        for s in ways:
            core.append(push(both(at[s, 2]), cdev))
        for s in ways:
            z3[s].wait_recv()
            z4[s] = push(one(at[s, 3], yl, s), zdev[s])
        yield
        for s in ways:
            z3b[s].wait_recv()
            z4b[s] = push(one(at[s, 3], 1 - yl, s), zdev[s])
            core.append(push(both(at[s, 3]), cdev))
        yield
        for s in ways:
            z4[s].wait_recv()
            z4b[s].wait_recv()
            core.append(push(both(at[s, 4], s), cdev))
        yield
        for copy in core:
            copy.wait_recv()

    def run(*gens):
        live = list(gens)
        while live:
            for g in list(live):
                if next(g, 1) == 1:
                    live.remove(g)

    half = pl.ds(pl.multiple_of((1 - yh) * HALF, HALF), HALF)
    normed, cots = gather(nrm, D), gather(ctg, D)
    next(normed)
    next(cots)
    seed = send(nrm.at[z, yl, c, :, half], ext.at[z, yl, c], hdev)

    def seeded():
        seed.wait_recv()
        yield from gather(ext, HALF)

    third = seeded()
    run(normed, cots)
    next(third)

    def tokens_of(buf, col, width):
        return buf[:, :, :, :, pl.ds(col, width)].reshape(NZ * 4 * ROWS, width)

    acc[...] = jnp.zeros_like(acc)

    def into(i, buf, weight):
        @pl.loop(0, D // TILE)
        def _(k):
            at = pl.multiple_of(k * TILE, TILE)
            acc[i] += lax.dot_general(
                tokens_of(buf, at, TILE), weight[:, pl.ds(at, TILE)], (((1,), (1,)), ((), ())),
                preferred_element_type=F32,
            )

    for load in loads:
        load.wait()
    into(0, nrm, wg)
    next(third)
    into(1, nrm, wu)
    next(third)

    @pl.loop(0, 4)
    def _(k):
        rows = pl.ds(pl.multiple_of(k * 128, 128), 128)
        gate, lifted = acc[0, rows, :], acc[1, rows, :]
        h = gate * jax.nn.sigmoid(gate) * lifted
        hid[rows, :] = h.astype(BF16)
        tra[pl.ds(0, W), rows] = h.T.astype(BF16)

    next(third)

    def down(other, xx):
        at = pl.multiple_of(other * HALF + xx * CH, CH)
        return jnp.dot(tra[pl.ds(0, W), :], tokens_of(ctg, at, CH), preferred_element_type=F32)

    def downs():
        far = (x + 2) % 4
        after, before = (x + 1) % 4, (x + 3) % 4
        vch[0] = down(0, far).astype(BF16)
        one = send(vch.at[0], vr1.at[0], xdev[1])
        vch[1] = down(1, far).astype(BF16)
        two = send(vch.at[1], vr1.at[1], xdev[-1])
        vch[2] = down(1, after).astype(BF16)
        three = send(vch.at[2], vr2.at[0, 1], xdev[1])
        vch[3] = down(0, before).astype(BF16)
        four = send(vch.at[3], vr2.at[1, 0], xdev[-1])
        yield
        vch[4] = down(0, after).astype(BF16)
        vch[5] = down(1, before).astype(BF16)
        yield
        one.wait_recv()
        vch[4] = (vch[4].astype(F32) + vr1[0].astype(F32)).astype(BF16)
        five = send(vch.at[4], vr2.at[0, 0], xdev[1])
        two.wait_recv()
        vch[5] = (vch[5].astype(F32) + vr1[1].astype(F32)).astype(BF16)
        six = send(vch.at[5], vr2.at[1, 1], xdev[-1])
        yield
        theirs, mine = down(1 - yh, x), down(yh, x)
        for copy in (three, four, five, six):
            copy.wait_recv()
        vst[...] = (theirs + vr2[0, 1 - yh].astype(F32) + vr2[1, 1 - yh].astype(F32)).astype(BF16)
        last = send(vst, vrecv, hdev)
        yield
        mine = mine + vr2[0, yh].astype(F32) + vr2[1, yh].astype(F32)
        last.wait_recv()
        wout[pl.ds(0, W), :] = (mine + vrecv[...].astype(F32)).astype(BF16)

    down_sum = downs()
    next(down_sum)
    next(third)

    @pl.loop(0, D // TILE)
    def _(k):
        at = pl.multiple_of(k * TILE, TILE)
        out = jnp.dot(hid[...], wd[:, pl.ds(at, TILE)], preferred_element_type=F32)
        part[0, :, :, :, :, pl.ds(at, TILE)] = out.astype(BF16).reshape(NZ, 2, 2, ROWS, TILE)

    def s2(s):
        return 0 if s == 1 else 1

    def scatter(i):
        theirs = part.at[i, pl.ds(0, NZ), pl.ds(0, 2), 1 - c]
        core = send(theirs, crecv.at[i], cdev)
        yield
        core.wait_recv()
        arrived = {}
        for h in range(4):
            for s in (1, -1):
                zz = (z + s * (4 - h) + NZ) % NZ
                if h == 0:
                    cols = pl.ds(0, D // 2) if s == 1 else pl.ds(D // 2, D // 2)
                    total = part[i, zz, :, c, :, cols].astype(F32) + crecv[i, zz, :, :, cols].astype(F32)
                    part[i, zz, :, c, :, cols] = total.astype(BF16)
                else:
                    arrived[s].wait_recv()
                    for cols, added in (
                        (pl.ds(0, D // 2), h > 1 or s == 1),
                        (pl.ds(D // 2, D // 2), h > 1 or s == -1),
                    ):
                        total = part[i, zz, :, c, :, cols].astype(F32) + crecv[i, zz, :, :, cols].astype(F32)
                        if added:
                            total = total + zrecv[i, s2(s), h - 1, :, :, cols].astype(F32)
                        part[i, zz, :, c, :, cols] = total.astype(BF16)
                    cols = pl.ds(0, D)
                arrived[s] = send(
                    part.at[i, zz, pl.ds(0, 2), c, :, cols],
                    zrecv.at[i, s2(s), h, pl.ds(0, 2), :, cols],
                    zdev[s],
                )
            yield
        for s in (1, -1):
            arrived[s].wait_recv()

        def total_of(y):
            return (
                part[i, z, y, c].astype(F32) + crecv[i, z, y].astype(F32)
                + zrecv[i, 0, 3, y].astype(F32) + zrecv[i, 1, 3, y].astype(F32)
            )

        yst[i] = total_of(1 - yl).astype(BF16)
        last = send(yst.at[i], yrecv.at[i], ydev)
        yield
        last.wait_recv()
        total = total_of(yl) + yrecv[i].astype(F32)
        xf, r, unit = normalized()
        if i == 0:
            mixed[...] = (xf + total).astype(BF16)
        else:
            gain = total * scale[...]
            inner = jnp.mean(gain * unit, axis=-1, keepdims=True)
            tgrad[...] = (cot[...].astype(F32) + r * (gain - unit * inner)).astype(BF16)

    forward = scatter(0)
    next(forward)
    next(third)
    into(2, ctg, wd)
    next(forward)
    next(third)

    @pl.loop(0, 4)
    def _(k):
        rows = pl.ds(pl.multiple_of(k * 128, 128), 128)
        gate, lifted, gh = acc[0, rows, :], acc[1, rows, :], acc[2, rows, :]
        sg = jax.nn.sigmoid(gate)
        gp = gh * lifted * sg * (1.0 + gate * (1.0 - sg))
        gl = gh * (gate * sg)
        gpr[rows, :] = gp.astype(BF16)
        glf[rows, :] = gl.astype(BF16)
        tra[pl.ds(W, W), rows] = gp.T.astype(BF16)
        tra[pl.ds(2 * W, W), rows] = gl.T.astype(BF16)

    swaps = []
    for g in range(2):
        rows = pl.ds((g + 1) * W, W)
        swaps.append(send(tra.at[rows], got.at[g], hdev))

    next(down_sum)

    @pl.loop(0, D // TILE)
    def _(k):
        at = pl.multiple_of(k * TILE, TILE)
        out = jnp.dot(gpr[...], wg[:, pl.ds(at, TILE)], preferred_element_type=F32)
        out += jnp.dot(glf[...], wu[:, pl.ds(at, TILE)], preferred_element_type=F32)
        part[1, :, :, :, :, pl.ds(at, TILE)] = out.astype(BF16).reshape(NZ, 2, 2, ROWS, TILE)

    backward = scatter(1)
    next(backward)
    run(third)
    next(forward)
    next(down_sum)
    next(backward)

    q = W // 2

    def weights(g, xx):
        at = pl.multiple_of(yh * HALF + xx * CH, CH)
        far = pl.multiple_of(xx * CH, CH)
        out = jnp.dot(tra[pl.ds((g + 1) * W, W), :], tokens_of(nrm, at, CH), preferred_element_type=F32)
        out += jnp.dot(got[g], tokens_of(ext, far, CH), preferred_element_type=F32)
        return out

    def over_x(g):
        up, down = pl.ds(0, q), pl.ds(q, q)
        swaps[g].wait_recv()
        far = (x + 2) % 4
        wch[g, 0] = weights(g, far).astype(BF16)
        one = send(wch.at[g, 0, up], xr1.at[g, 0], xdev[1])
        two = send(wch.at[g, 0, down], xr1.at[g, 1], xdev[-1])
        wch[g, 1] = weights(g, (x + 1) % 4).astype(BF16)
        three = send(wch.at[g, 1, down], xr2.at[g, 0, down], xdev[1])
        wch[g, 2] = weights(g, (x + 3) % 4).astype(BF16)
        four = send(wch.at[g, 2, up], xr2.at[g, 1, up], xdev[-1])
        yield
        one.wait_recv()
        wch[g, 1, up] = (wch[g, 1, up].astype(F32) + xr1[g, 0].astype(F32)).astype(BF16)
        five = send(wch.at[g, 1, up], xr2.at[g, 0, up], xdev[1])
        two.wait_recv()
        wch[g, 2, down] = (wch[g, 2, down].astype(F32) + xr1[g, 1].astype(F32)).astype(BF16)
        six = send(wch.at[g, 2, down], xr2.at[g, 1, down], xdev[-1])
        yield
        mine = weights(g, x)
        for copy in (three, four, five, six):
            copy.wait_recv()
        total = mine + xr2[g, 0].astype(F32) + xr2[g, 1].astype(F32)
        wout[pl.ds((g + 1) * W, W), :] = total.astype(BF16)

    gate_sum, up_sum = over_x(0), over_x(1)
    next(forward)
    next(backward)
    next(gate_sum)
    next(forward)
    next(backward)
    next(up_sum)
    next(down_sum)
    next(forward)
    next(backward)
    next(gate_sum)
    run(forward)
    next(backward)
    run(down_sum)
    next(up_sum)
    run(backward)
    run(gate_sum)
    run(up_sum)

    for copy in sent:
        copy.wait_send()


def finish(mixed, tgrad, wout, mixed_out, tgrad_out, gate_out, up_out, down_out):
    mixed_out[...] = mixed[...]
    tgrad_out[...] = tgrad[...]
    gate_out[...] = wout[W : 2 * W]
    up_out[...] = wout[2 * W :]
    down_out[...] = wout[:W]


def local(tokens, norm_scale_vector, gate_weight, up_weight, down_weight, cotangent):
    vmem = pl.BlockSpec(memory_space=pltpu.VMEM)
    hbm = pl.BlockSpec(memory_space=pl.ANY)
    slab = (NZ, 2, 2, ROWS, D)
    count = 128
    mixed, tgrad, wout = pl.pallas_call(
        kernel,
        out_shape=(
            jax.ShapeDtypeStruct((ROWS, D), BF16),
            jax.ShapeDtypeStruct((ROWS, D), BF16),
            jax.ShapeDtypeStruct((3 * W, CH), BF16),
        ),
        in_specs=[vmem, vmem, vmem, hbm, hbm, hbm],
        out_specs=(vmem, vmem, vmem),
        scratch_shapes=[
            pltpu.VMEM(slab, BF16),
            pltpu.VMEM(slab, BF16),
            pltpu.VMEM((NZ, 2, 2, ROWS, HALF), BF16),
            pltpu.VMEM((W, D), BF16),
            pltpu.VMEM((W, D), BF16),
            pltpu.VMEM((W, D), BF16),
            pltpu.VMEM((3, 512, W), F32),
            pltpu.VMEM((512, W), BF16),
            pltpu.VMEM((512, W), BF16),
            pltpu.VMEM((512, W), BF16),
            pltpu.VMEM((3 * W, 512), BF16),
            pltpu.VMEM((2, W, 512), BF16),
            pltpu.VMEM((2, *slab), BF16),
            pltpu.VMEM((2, NZ, 2, ROWS, D), BF16),
            pltpu.VMEM((2, 2, 4, 2, ROWS, D), BF16),
            pltpu.VMEM((2, ROWS, D), BF16),
            pltpu.VMEM((2, ROWS, D), BF16),
            pltpu.VMEM((6, W, CH), BF16),
            pltpu.VMEM((2, W, CH), BF16),
            pltpu.VMEM((2, 2, W, CH), BF16),
            pltpu.VMEM((W, CH), BF16),
            pltpu.VMEM((W, CH), BF16),
            pltpu.VMEM((2, 3, W, CH), BF16),
            pltpu.VMEM((2, 2, W // 2, CH), BF16),
            pltpu.VMEM((2, 2, W, CH), BF16),
            pltpu.SemaphoreType.DMA((3,)),
            pltpu.SemaphoreType.DMA((count,)),
            pltpu.SemaphoreType.DMA((count,)),
        ],
        compiler_params=pltpu.CompilerParams(
            collective_id=0, has_side_effects=True, vmem_limit_bytes=62 << 20
        ),
        cost_estimate=pl.CostEstimate(
            flops=2 * 9 * 512 * D * W, bytes_accessed=16 << 20, transcendentals=512 * W
        ),
        name="ffn",
    )(tokens, norm_scale_vector.reshape(1, D), cotangent, gate_weight.T, up_weight.T, down_weight)
    block = jax.ShapeDtypeStruct((W, CH), BF16)
    mixed, tgrad, gate, up, down = pl.pallas_call(
        finish,
        out_shape=(*(jax.ShapeDtypeStruct(v.shape, v.dtype) for v in (mixed, tgrad)), block, block, block),
        in_specs=[vmem] * 3,
        out_specs=(vmem,) * 5,
        compiler_params=pltpu.CompilerParams(vmem_limit_bytes=62 << 20),
        name="finish",
    )(mixed, tgrad, wout)
    return mixed, tgrad, gate.T, up.T, down


def solution(mesh):
    both, rows = P(("dp", "tp"), None), P()
    return jax.shard_map(
        local,
        mesh=mesh,
        in_specs=(both, rows, P(None, "tp"), P(None, "tp"), P("tp", None), both),
        out_specs=(both, both, P("dp", "tp"), P("dp", "tp"), P("tp", "dp")),
        check_vma=False,
    )
```

time: 175 us -> 134 us (0.77)
  Pallas kernels: 156 us -> 133 us
  local copies, waits for them, and re-layouts: 18.4 us -> 0 us
    pallas_call x1, Pallas kernels: 156 us -> 130 us  [local(): pl.pallas_call(kernel, out_shape=(jax.ShapeDtypeStruct((ROWS, D), BF16),...]
    unnamed x4 -> x0, local copies, waits for them, and re-layouts: 16 us -> none
    pallas_call x0 -> x1, Pallas kernels: none -> 2.65 us  [local(): pl.pallas_call(finish, out_shape=(*(jax.ShapeDtypeStruct(v.shape, v.dtype...]
    slice x1 -> x0, local copies, waits for them, and re-layouts: 2.4 us -> none  [local(): return (mixed, tgrad, wout[W:2 * W].T, wout[2 * W:].T, wout[:W])]
where the time goes in v2:
time: 134 us
  Pallas kernels  133 us (99%)
    pallas_call x1, Pallas kernels, local(): pl.pallas_call(kernel, out_shape=(jax.ShapeDtypeStruct((ROWS, D), BF16),...  130 us

profile of v2, /device:TPU:1, one launch (start us, length us, event | category | flops | bytes accessed | tf_op | source)
XLA Modules:
  0.0 133.5 jit_solution(14650520523630235054)
XLA Ops:
  0.6 130.2 %ffn.1 = (bf16[16,4096]{1,0:T(8,128)(2,1)}, bf16[16,4096]{1,0:T(8,128)(2,1)}, bf16[1344,512]{1,0:T(8,128)(2,1)}) custom-call(bf16[16,4096]{1,0:T(8,128)(2,1)} %tok.1, f32[1,4096]{1,0:T(1,128)} %bitcast.9, bf16[16,4096]{1,0:T(8,128)(2,1)} %cot.1, bf16[448,4096]{1,0:T(8,128)(2,1)} %bitcast.5, bf16[448,4096]{1,0:T(8,128)(2,1)} %bitcast.6, bf16[448,4096]{1,0:T(8,128)(2,1)} %dw.1), custom_call_target="tpu_custom_call" | custom-call | flops 16911433728 | bytes 16777216 | tf_op jit(solution)/shard_map/ffn/pallas_call | solution.py:393
  130.8 2.7 %finish.1 = (bf16[16,4096]{1,0:T(8,128)(2,1)}, bf16[16,4096]{1,0:T(8,128)(2,1)}, bf16[448,512]{1,0:T(8,128)(2,1)}, bf16[448,512]{1,0:T(8,128)(2,1)}, bf16[448,512]{1,0:T(8,128)(2,1)}) custom-call(bf16[16,4096]{1,0:T(8,128)(2,1)} %get-tuple-element.13.mixed, bf16[16,4096]{1,0:T(8,128)(2,1)} %get-tuple-element.14.tgrad, bf16[1344,512]{1,0:T(8,128)(2,1)} %get-tuple-element.15.wout), custom_call_target="tpu_custom_call" | custom-call | tf_op jit(solution)/shard_map/finish/pallas_call | solution.py:441

commit v3 on v2

--- a/solution.py
+++ b/solution.py
@@ -17,6 +17,7 @@
 HALF = 2048
 CH = 512
 TILE = 512
+DEPTH = 2048
 
 
 def kernel(
@@ -67,15 +68,15 @@
     ctg[z, yl, c] = cot[...]
     pl.semaphore_wait(barrier, len(partners))
 
-    def gather(buf, width):
+    def gather(buf, width, base=0):
         def one(zz, y, s=0):
             mid = width // 2
-            cols = {0: pl.ds(0, width), 1: pl.ds(0, mid), -1: pl.ds(mid, mid)}[s]
+            cols = {0: pl.ds(base, width), 1: pl.ds(base, mid), -1: pl.ds(base + mid, mid)}[s]
             return buf.at[zz, y, c, :, cols]
 
         def both(zz, s=0):
             mid = width // 2
-            cols = {0: pl.ds(0, width), 1: pl.ds(0, mid), -1: pl.ds(mid, mid)}[s]
+            cols = {0: pl.ds(base, width), 1: pl.ds(base, mid), -1: pl.ds(base + mid, mid)}[s]
             return buf.at[zz, pl.ds(0, 2), c, :, cols]
 
         def push(ref, device):
@@ -90,7 +91,6 @@
         for s in ways:
             z1[s].wait_recv()
             z2[s] = push(one(at[s, 1], yl), zdev[s])
-            y1[s] = push(one(at[s, 1], yl), ydev)
         yield
         y0.wait_recv()
         core = [push(both(z), cdev)]
@@ -101,19 +101,21 @@
             y2[s] = push(one(at[s, 2], yl), ydev)
         yield
         for s in ways:
+            y1[s] = push(one(at[s, 1], yl), ydev)
+        for s in ways:
+            y2[s].wait_recv()
+            z3b[s] = push(one(at[s, 2], 1 - yl), zdev[s])
+        yield
+        z4, z4b = {}, {}
+        for s in ways:
+            core.append(push(both(at[s, 2]), cdev))
+        for s in ways:
+            z3[s].wait_recv()
+            z4[s] = push(one(at[s, 3], yl, s), zdev[s])
+        yield
+        for s in ways:
             y1[s].wait_recv()
             core.append(push(both(at[s, 1]), cdev))
-        for s in ways:
-            y2[s].wait_recv()
-            z3b[s] = push(one(at[s, 2], 1 - yl), zdev[s])
-        yield
-        z4, z4b = {}, {}
-        for s in ways:
-            core.append(push(both(at[s, 2]), cdev))
-        for s in ways:
-            z3[s].wait_recv()
-            z4[s] = push(one(at[s, 3], yl, s), zdev[s])
-        yield
         for s in ways:
             z3b[s].wait_recv()
             z4b[s] = push(one(at[s, 3], 1 - yl, s), zdev[s])
@@ -123,6 +125,62 @@
             z4[s].wait_recv()
             z4b[s].wait_recv()
             core.append(push(both(at[s, 4], s), cdev))
+        yield
+        for copy in core:
+            copy.wait_recv()
+
+    def gather_pairs(buf, width, base=0):
+        mid = width // 2
+
+        def rows(zz, y, s=0):
+            cols = {0: pl.ds(base, width), 1: pl.ds(base, mid), -1: pl.ds(base + mid, mid)}[s]
+            return buf.at[zz, y, c, :, cols]
+
+        def push(ref, device):
+            return send(ref, ref, device)
+
+        at = {(s, h): (z - s * h + NZ) % NZ for s in (1, -1) for h in (1, 2, 3, 4)}
+        ways, core, own, other = (1, -1), [], {}, {}
+
+        def on(zz, h, y, got):
+            for s in ways:
+                if h > 0:
+                    got[s].wait_recv()
+                place = zz if h == 0 else at[s, h]
+                got[s] = push(rows(place, y, s if h == 3 else 0), zdev[s])
+
+        def across(h, s, half=0):
+            cols = {0: pl.ds(base, width), 1: pl.ds(base, mid), -1: pl.ds(base + mid, mid)}[half]
+            ref = buf.at[z if h == 0 else at[s, h], pl.ds(0, 2), c, :, cols]
+            core.append(push(ref, cdev))
+
+        y0 = push(rows(z, yl), ydev)
+        on(z, 0, yl, own)
+        yield
+        y0.wait_recv()
+        on(z, 0, 1 - yl, other)
+        across(0, 1)
+        yield
+        on(z, 1, yl, own)
+        yield
+        on(z, 1, 1 - yl, other)
+        for s in ways:
+            across(1, s)
+        on(z, 2, yl, own)
+        yield
+        on(z, 2, 1 - yl, other)
+        for s in ways:
+            across(2, s)
+        yield
+        on(z, 3, yl, own)
+        on(z, 3, 1 - yl, other)
+        for s in ways:
+            across(3, s)
+        yield
+        for s in ways:
+            own[s].wait_recv()
+            other[s].wait_recv()
+            across(4, s, s)
         yield
         for copy in core:
             copy.wait_recv()
@@ -135,17 +193,19 @@
                     live.remove(g)
 
     half = pl.ds(pl.multiple_of((1 - yh) * HALF, HALF), HALF)
-    normed, cots = gather(nrm, D), gather(ctg, D)
-    next(normed)
-    next(cots)
+    most = 3584
+    both_ways = [gather(buf, most) for buf in (nrm, ctg)]
+    both_ways += [gather_pairs(buf, D - most, most) for buf in (nrm, ctg)]
+    for way in both_ways:
+        next(way)
     seed = send(nrm.at[z, yl, c, :, half], ext.at[z, yl, c], hdev)
 
     def seeded():
         seed.wait_recv()
-        yield from gather(ext, HALF)
+        yield from gather_pairs(ext, HALF)
 
     third = seeded()
-    run(normed, cots)
+    run(*both_ways)
     next(third)
 
     def tokens_of(buf, col, width):
@@ -154,11 +214,11 @@
     acc[...] = jnp.zeros_like(acc)
 
     def into(i, buf, weight):
-        @pl.loop(0, D // TILE)
+        @pl.loop(0, D // DEPTH)
         def _(k):
-            at = pl.multiple_of(k * TILE, TILE)
+            at = pl.multiple_of(k * DEPTH, DEPTH)
             acc[i] += lax.dot_general(
-                tokens_of(buf, at, TILE), weight[:, pl.ds(at, TILE)], (((1,), (1,)), ((), ())),
+                tokens_of(buf, at, DEPTH), weight[:, pl.ds(at, DEPTH)], (((1,), (1,)), ((), ())),
                 preferred_element_type=F32,
             )
 
@@ -389,7 +449,7 @@
     vmem = pl.BlockSpec(memory_space=pltpu.VMEM)
     hbm = pl.BlockSpec(memory_space=pl.ANY)
     slab = (NZ, 2, 2, ROWS, D)
-    count = 128
+    count = 216
     mixed, tgrad, wout = pl.pallas_call(
         kernel,
         out_shape=(

time: 134 us -> 128 us (0.955)
  Pallas kernels: 133 us -> 127 us
    pallas_call x1, Pallas kernels: 130 us -> 124 us  [local(): pl.pallas_call(kernel, out_shape=(jax.ShapeDtypeStruct((ROWS, D), BF16),...]
where the time goes in v3:
time: 128 us
  Pallas kernels  127 us (99%)
    pallas_call x1, Pallas kernels, local(): pl.pallas_call(kernel, out_shape=(jax.ShapeDtypeStruct((ROWS, D), BF16),...  124 us
    pallas_call x1, Pallas kernels, local(): pl.pallas_call(finish, out_shape=(*(jax.ShapeDtypeStruct(v.shape, v.dtype...  2.65 us

profile of v3, /device:TPU:1, one launch (start us, length us, event | category | flops | bytes accessed | tf_op | source)
XLA Modules:
  0.0 127.7 jit_solution(14904951561675923140)
XLA Ops:
  0.6 124.4 %ffn.1 = (bf16[16,4096]{1,0:T(8,128)(2,1)}, bf16[16,4096]{1,0:T(8,128)(2,1)}, bf16[1344,512]{1,0:T(8,128)(2,1)}) custom-call(bf16[16,4096]{1,0:T(8,128)(2,1)} %tok.1, f32[1,4096]{1,0:T(1,128)} %bitcast.9, bf16[16,4096]{1,0:T(8,128)(2,1)} %cot.1, bf16[448,4096]{1,0:T(8,128)(2,1)} %bitcast.5, bf16[448,4096]{1,0:T(8,128)(2,1)} %bitcast.6, bf16[448,4096]{1,0:T(8,128)(2,1)} %dw.1), custom_call_target="tpu_custom_call" | custom-call | flops 16911433728 | bytes 16777216 | tf_op jit(solution)/shard_map/ffn/pallas_call | solution.py:453
  125.0 2.7 %finish.1 = (bf16[16,4096]{1,0:T(8,128)(2,1)}, bf16[16,4096]{1,0:T(8,128)(2,1)}, bf16[448,512]{1,0:T(8,128)(2,1)}, bf16[448,512]{1,0:T(8,128)(2,1)}, bf16[448,512]{1,0:T(8,128)(2,1)}) custom-call(bf16[16,4096]{1,0:T(8,128)(2,1)} %get-tuple-element.13.mixed, bf16[16,4096]{1,0:T(8,128)(2,1)} %get-tuple-element.14.tgrad, bf16[1344,512]{1,0:T(8,128)(2,1)} %get-tuple-element.15.wout), custom_call_target="tpu_custom_call" | custom-call | tf_op jit(solution)/shard_map/finish/pallas_call | solution.py:501

commit v4 on v3

--- a/solution.py
+++ b/solution.py
@@ -211,16 +211,16 @@
     def tokens_of(buf, col, width):
         return buf[:, :, :, :, pl.ds(col, width)].reshape(NZ * 4 * ROWS, width)
 
-    acc[...] = jnp.zeros_like(acc)
-
     def into(i, buf, weight):
-        @pl.loop(0, D // DEPTH)
-        def _(k):
-            at = pl.multiple_of(k * DEPTH, DEPTH)
-            acc[i] += lax.dot_general(
-                tokens_of(buf, at, DEPTH), weight[:, pl.ds(at, DEPTH)], (((1,), (1,)), ((), ())),
+        dims = (((1,), (1,)), ((), ()))
+        first, second = (
+            lax.dot_general(
+                tokens_of(buf, at, DEPTH), weight[:, pl.ds(at, DEPTH)], dims,
                 preferred_element_type=F32,
             )
+            for at in (0, DEPTH)
+        )
+        acc[i] = first + second
 
     for load in loads:
         load.wait()

time: 128 us -> 127 us (level)
  no operation moved by 1% of the time
where the time goes in v4:
time: 127 us
  Pallas kernels  126 us (99%)
    pallas_call x1, Pallas kernels, local(): pl.pallas_call(kernel, out_shape=(jax.ShapeDtypeStruct((ROWS, D), BF16),...  124 us
    pallas_call x1, Pallas kernels, local(): pl.pallas_call(finish, out_shape=(*(jax.ShapeDtypeStruct(v.shape, v.dtype...  2.65 us

profile of v4, /device:TPU:1, one launch (start us, length us, event | category | flops | bytes accessed | tf_op | source)
XLA Modules:
  0.0 127.1 jit_solution(3445012078690318799)
XLA Ops:
  0.6 123.8 %ffn.1 = (bf16[16,4096]{1,0:T(8,128)(2,1)}, bf16[16,4096]{1,0:T(8,128)(2,1)}, bf16[1344,512]{1,0:T(8,128)(2,1)}) custom-call(bf16[16,4096]{1,0:T(8,128)(2,1)} %tok.1, f32[1,4096]{1,0:T(1,128)} %bitcast.9, bf16[16,4096]{1,0:T(8,128)(2,1)} %cot.1, bf16[448,4096]{1,0:T(8,128)(2,1)} %bitcast.5, bf16[448,4096]{1,0:T(8,128)(2,1)} %bitcast.6, bf16[448,4096]{1,0:T(8,128)(2,1)} %dw.1), custom_call_target="tpu_custom_call" | custom-call | flops 16911433728 | bytes 16777216 | tf_op jit(solution)/shard_map/ffn/pallas_call | solution.py:453
  124.4 2.7 %finish.1 = (bf16[16,4096]{1,0:T(8,128)(2,1)}, bf16[16,4096]{1,0:T(8,128)(2,1)}, bf16[448,512]{1,0:T(8,128)(2,1)}, bf16[448,512]{1,0:T(8,128)(2,1)}, bf16[448,512]{1,0:T(8,128)(2,1)}) custom-call(bf16[16,4096]{1,0:T(8,128)(2,1)} %get-tuple-element.13.mixed, bf16[16,4096]{1,0:T(8,128)(2,1)} %get-tuple-element.14.tgrad, bf16[1344,512]{1,0:T(8,128)(2,1)} %get-tuple-element.15.wout), custom_call_target="tpu_custom_call" | custom-call | tf_op jit(solution)/shard_map/finish/pallas_call | solution.py:501
